TPU v7x, 512 devices: a whole 4x8x8 slice. The times are simulated.
512 devices in a mesh: streams: 16 (over y, core), tp: 32 (over x, z).
Axes of the slice: x: 4, y: 8, z: 8, core: 2. Of those that a mesh axis runs over, the one named last changes fastest.
Arguments:
- hidden_in: bfloat16 [512, 4, 1024], P(('streams', 'tp')), may hold values from -6 to 6
- byte_qkv: bfloat16 [512, 4, 1536], P(('streams', 'tp'))
- byte_cache: bfloat16 [512, 256, 512], P(('streams', 'tp'))
- byte_len: int32 [512], P(('streams', 'tp')), may hold values from 2 to 256, as said below
- flags: int32 [512, 4], P(('streams', 'tp')), may hold values 0 or 1
- coarse_prev: bfloat16 [512, 1024], P(('streams', 'tp')), may hold values from -6 to 6
- owner_map: int32 [32, 16, 1], replicated, may hold values from 0 to 15; in each aligned block of 16 rows (0 to 15, 16 to 31, ..., all dimensions but the last counted through in order) at most 2 rows name the same one
- up_weight: bfloat16 [1024, 8192], P(None, 'tp'), may hold values from -0.1875 to 0.1875
- coarse_gain: float32 [8192], replicated, may hold values from 0.5 to 1.5
- query_weight: bfloat16 [8192, 4096], P(None, 'tp'), may hold values from -0.0625 to 0.0625
- keyval_weight: bfloat16 [8192, 1024], P('tp'), may hold values from -0.0625 to 0.0625
- return_weight: bfloat16 [4096, 1024], P('tp'), may hold values from -0.09375 to 0.09375
- coarse_cache: bfloat16 [16, 64, 32, 32, 256], P('streams', None, 'tp'), as said below
- coarse_len: int32 [16, 64], P('streams'), may hold values from 1 to 32, as said below
Outputs:
- byte_out: bfloat16 [512, 4, 1024], P(('streams', 'tp'))
Inputs may be any that keep to these rules, and one draw needn't show every extreme that they name: `owner_map`: within one index c of tp, no group owns more than 2 of the sequences s * 32 + c, and some group owns exactly 2. `byte_len`: some sequence has exactly 256 filled positions. `coarse_len`: some slot has exactly 32 filled positions. `coarse_cache`: the copies for heads h and h2 are equal where h // 8 = h2 // 8.
All inputs are finite; a program needn't handle non-finite values. No bound on the sum of `flags` on one device may be relied on, other than what follows from the above.
Results may differ from a plain program's by a relative error of at most 0.014.
Values may be sent and summed in bfloat16 or wider, within the bound.
A program may use at most 64 MiB of HBM per device.

v0:
```python
import jax
import jax.numpy as jnp
from jax import lax
from jax.sharding import PartitionSpec as P

HD = 128
OWNED_MOST = 2
EPSILON = 1e-05
NEG_FILL = -1e30


def split_softmax(scores_old, scores_new):
    largest = jnp.maximum(
        jnp.max(scores_old, axis=-1, keepdims=True), jnp.max(scores_new, axis=-1, keepdims=True)
    )
    exp_old = jnp.exp(scores_old - largest)
    exp_new = jnp.exp(scores_new - largest)
    denominator = jnp.sum(exp_old, axis=-1, keepdims=True) + jnp.sum(
        exp_new, axis=-1, keepdims=True
    )
    return (
        (exp_old / denominator).astype(jnp.bfloat16),
        (exp_new / denominator).astype(jnp.bfloat16),
    )


def rank_table(owner_map):
    owners = owner_map[:, :, 0]
    group_total = owners.shape[1]
    same_owner = owners[:, :, None] == owners[:, None, :]
    earlier = (
        jnp.arange(group_total, dtype=jnp.int32)[None, :, None]
        > jnp.arange(group_total, dtype=jnp.int32)[None, None, :]
    )
    ranking = jnp.sum((same_owner & earlier).astype(jnp.int32), axis=2)
    return (owners, ranking)


def byte_attention(byte_qkv, byte_cache, byte_len):
    number, step_count, total_width = byte_qkv.shape
    length = byte_cache.shape[1]
    kv_width = byte_cache.shape[2] // 2
    kv_groups = kv_width // HD
    head_count = (total_width - 2 * kv_width) // HD
    group_size = head_count // kv_groups
    query_part = byte_qkv[:, :, : head_count * HD].reshape(
        number, step_count, kv_groups, group_size, HD
    )
    new_keys = byte_qkv[:, :, head_count * HD : head_count * HD + kv_width].reshape(
        number, step_count, kv_groups, HD
    )
    new_values = byte_qkv[:, :, head_count * HD + kv_width :].reshape(
        number, step_count, kv_groups, HD
    )
    old_keys = byte_cache[:, :, :kv_width].reshape(number, length, kv_groups, HD)
    old_values = byte_cache[:, :, kv_width:].reshape(number, length, kv_groups, HD)
    scaling = HD ** (-0.5)
    scores_old = (
        jnp.einsum("nsgjd,nlgd->nsgjl", query_part, old_keys, preferred_element_type=jnp.float32)
        * scaling
    )
    valid_old = jnp.arange(length, dtype=jnp.int32)[None, :] < byte_len[:, None]
    scores_old = jnp.where(valid_old[:, None, None, None, :], scores_old, NEG_FILL)
    scores_new = (
        jnp.einsum("nsgjd,nugd->nsgju", query_part, new_keys, preferred_element_type=jnp.float32)
        * scaling
    )
    causal = jnp.arange(step_count)[:, None] >= jnp.arange(step_count)[None, :]
    scores_new = jnp.where(causal[None, :, None, None, :], scores_new, NEG_FILL)
    weights_old, weights_new = split_softmax(scores_old, scores_new)
    mixed_heads = jnp.einsum(
        "nsgjl,nlgd->nsgjd", weights_old, old_values, preferred_element_type=jnp.float32
    )
    mixed_heads = mixed_heads + jnp.einsum(
        "nsgju,nugd->nsgjd", weights_new, new_values, preferred_element_type=jnp.float32
    )
    return mixed_heads.reshape(number, step_count, head_count * HD)


def dispatch(block_rows, block_marks, owners, ranking):
    column_total = lax.axis_size("tp")
    row_index = lax.axis_index("streams")
    every_rows, every_marks = (
        lax.all_gather(block_rows, ("streams", "tp"), axis=0, tiled=True),
        lax.all_gather(block_marks, ("streams", "tp"), axis=0, tiled=True),
    )
    target = jnp.where(
        owners == row_index,
        jnp.arange(column_total, dtype=jnp.int32)[:, None] * OWNED_MOST + ranking,
        -1,
    )
    target_flat = target.T.reshape(-1)
    slot_ids = jnp.arange(column_total * OWNED_MOST, dtype=jnp.int32)
    picker = (slot_ids[:, None] == target_flat[None, :]).astype(jnp.bfloat16)
    slot_rows = jnp.einsum(
        "ai,ibd->abd", picker, every_rows, preferred_element_type=jnp.float32
    ).astype(jnp.bfloat16)
    slot_marks = jnp.einsum("ai,ib->ab", picker, every_marks, preferred_element_type=jnp.float32)
    return (slot_rows, slot_marks)


def coarse_project(slot_rows, up_weight, coarse_gain, query_weight, keyval_weight):
    column_total = lax.axis_size("tp")
    column = lax.axis_index("tp")
    part_width = up_weight.shape[1]
    expanded = jnp.einsum(
        "rbd,df->rbf", slot_rows, up_weight, preferred_element_type=jnp.float32
    ).astype(jnp.bfloat16)
    widened = lax.all_gather(expanded, "tp", axis=2, tiled=True).astype(jnp.float32)
    scaled_part = (widened * coarse_gain).astype(jnp.bfloat16)
    query_sum = jnp.einsum(
        "rbf,fh->rbh", scaled_part, query_weight, preferred_element_type=jnp.float32
    )
    squares = jnp.sum(widened * widened, axis=2)
    query_sum, squares = (query_sum, squares)
    own_gains = lax.dynamic_slice_in_dim(coarse_gain, column * part_width, part_width, 0)
    own_scaled = (expanded.astype(jnp.float32) * own_gains).astype(jnp.bfloat16)
    inverse = lax.rsqrt(squares / (part_width * column_total) + EPSILON)[:, :, None]
    queries = (query_sum * inverse).astype(jnp.bfloat16)
    kv_width = keyval_weight.shape[1]
    kv_heads = kv_width // (2 * HD)
    group_size = column_total // kv_heads
    head_group = column // group_size
    keyval_part = jnp.einsum(
        "rbf,fc->rbc", own_scaled, keyval_weight, preferred_element_type=jnp.float32
    )
    keyvals = lax.psum(keyval_part, "tp")
    new_keys = (lax.dynamic_slice_in_dim(keyvals, head_group * HD, HD, 2) * inverse).astype(
        jnp.bfloat16
    )
    new_values = (
        lax.dynamic_slice_in_dim(keyvals, (kv_heads + head_group) * HD, HD, 2) * inverse
    ).astype(jnp.bfloat16)
    return (queries, new_keys, new_values)


def coarse_attention(queries, step_ids, cache_own, cache_len, key_store, value_store, mark_store):
    length = cache_own.shape[1]
    step_count = key_store.shape[1]
    scaling = HD ** (-0.5)
    scores_old = (
        jnp.einsum(
            "rbd,rld->rbl", queries, cache_own[:, :, :HD], preferred_element_type=jnp.float32
        )
        * scaling
    )
    valid_old = jnp.arange(length, dtype=jnp.int32)[None, :] < cache_len[:, None]
    scores_old = jnp.where(valid_old[:, None, :], scores_old, NEG_FILL)
    scores_new = (
        jnp.einsum("rbd,rud->rbu", queries, key_store, preferred_element_type=jnp.float32) * scaling
    )
    valid_new = (jnp.arange(step_count)[None, None, :] <= step_ids[None, :, None]) & (
        mark_store[:, None, :] > 0.5
    )
    scores_new = jnp.where(valid_new, scores_new, NEG_FILL)
    weights_old, weights_new = split_softmax(scores_old, scores_new)
    mixed_heads = jnp.einsum(
        "rbl,rld->rbd", weights_old, cache_own[:, :, HD:], preferred_element_type=jnp.float32
    )
    mixed_heads = mixed_heads + jnp.einsum(
        "rbu,rud->rbd", weights_new, value_store, preferred_element_type=jnp.float32
    )
    return mixed_heads.astype(jnp.bfloat16)


def give_back(mixed_heads, return_weight, owners, ranking):
    row_index = lax.axis_index("streams")
    column = lax.axis_index("tp")
    summed = lax.psum_scatter(
        jnp.einsum("rbh,hd->rbd", mixed_heads, return_weight, preferred_element_type=jnp.float32),
        "tp",
        scatter_dimension=0,
        tiled=True,
    ).astype(jnp.bfloat16)
    every_back = lax.all_gather(summed, "streams", axis=0, tiled=True)
    my_owner = lax.dynamic_index_in_dim(
        lax.dynamic_index_in_dim(owners, column, 0, keepdims=False), row_index, 0, keepdims=False
    )
    my_rank = lax.dynamic_index_in_dim(
        lax.dynamic_index_in_dim(ranking, column, 0, keepdims=False), row_index, 0, keepdims=False
    )
    return lax.dynamic_index_in_dim(every_back, my_owner * OWNED_MOST + my_rank, 0, keepdims=False)


def shards(
    hidden_in,
    byte_qkv,
    byte_cache,
    byte_len,
    flags,
    coarse_prev,
    owner_map,
    up_weight,
    coarse_gain,
    query_weight,
    keyval_weight,
    return_weight,
    coarse_cache,
    coarse_len,
):
    step_count = hidden_in.shape[1]
    attended = byte_attention(byte_qkv, byte_cache, byte_len)
    byte_rows = (hidden_in.astype(jnp.float32) + attended).astype(jnp.bfloat16)
    byte_marks = flags.astype(jnp.bfloat16)
    owners, ranking = rank_table(owner_map)
    cache_own = coarse_cache[0, :, 0]
    cache_len = coarse_len[0]
    slot_rows, slot_marks = dispatch(byte_rows, byte_marks, owners, ranking)
    queries, new_keys, new_values = coarse_project(
        slot_rows, up_weight, coarse_gain, query_weight, keyval_weight
    )
    step_ids = jnp.arange(step_count, dtype=jnp.int32)
    mixed_heads = coarse_attention(
        queries, step_ids, cache_own, cache_len, new_keys, new_values, slot_marks
    )
    given_back = give_back(mixed_heads, return_weight, owners, ranking)
    current = coarse_prev[0].astype(jnp.float32)
    outputs = []
    for step in range(step_count):
        current = jnp.where(flags[0, step] > 0, given_back[step].astype(jnp.float32), current)
        outputs.append(byte_rows[0, step].astype(jnp.float32) + current)
    return jnp.stack(outputs)[None].astype(jnp.bfloat16)


def solution(mesh):
    return jax.shard_map(
        shards,
        mesh=mesh,
        in_specs=(
            P(("streams", "tp"), None, None),
            P(("streams", "tp"), None, None),
            P(("streams", "tp"), None, None),
            P(("streams", "tp")),
            P(("streams", "tp"), None),
            P(("streams", "tp"), None),
            P(),
            P(None, "tp"),
            P(),
            P(None, "tp"),
            P("tp", None),
            P("tp", None),
            P("streams", None, "tp", None, None),
            P("streams", None),
        ),
        out_specs=P(("streams", "tp"), None, None),
        check_vma=False,
    )
```

profile of v0, /device:TPU:1, one launch (start us, length us, event | category | flops | bytes accessed | tf_op | source)
XLA Modules:
  0.0 587.4 jit_solution(7376833832583837293)
XLA Ops:
  6.6 1.1 fusion.96
  7.9 0.7 slice.62
  9.3 0.9 convolution_multiply_fusion.2
  11.1 0.9 fusion.32
  12.0 0.7 fusion.61
  13.4 0.9 convert_reduce_fusion
  14.3 0.7 select_bitcast_fusion
  15.1 122.9 %all-gather.4.cloned.1.call-done = bf16[512,4,1024]{2,1,0:T(4,128)(2,1)} async-done(((bf16[1,4,1024]{2,1,0:T(4,128)(2,1)}), bf16[512,4,1024]{2,1,0:T(4,128)(2,1)}) %all-gather.4.cloned.1.call-update) | async-done | bytes 4194320 | tf_op jit(solution)/shard_map/all_gather | solution.py:84
  138.0 5.7 fusion.14
  143.8 1.2 fusion.100
  146.9 90.5 %all-gather = bf16[512,1,4]{2,1,0:T(2,128)(2,1)S(1)} all-gather(bf16[1,1,4]{2,1,0:T(2,128)(2,1)S(1)} %convert_bitcast_fusion), channel_id=1, replica_groups=mesh['streams'=16,'tp'=32] {'streams','tp'}, dimensions={0}, use_global_device_ids=true | all-gather | bytes 4104 | tf_op jit(solution)/shard_map/all_gather | solution.py:85
  237.6 0.7 fusion.97
  240.9 1.3 dynamic-slice.4
  243.1 2.2 fusion.35
  245.4 3.3 fusion.1
  248.8 1.2 fusion.23
  250.1 148.3 %all-reduce.4.cloned.1.call-done = f32[64,4,1024]{2,0,1:T(8,128)} async-done(((f32[64,4,1024]{2,0,1:T(8,128)}), f32[64,4,1024]{2,0,1:T(8,128)}) %all-reduce.4.cloned.1.call-update) | async-done | bytes 1048592 | tf_op jit(solution)/shard_map/psum | solution.py:127
  398.4 1.1 multiply_convert_fusion.2
  400.0 1.5 fusion.99
  402.5 1.4 fusion.28
  404.2 0.7 copy.161
  404.9 125.0 %all-reduce.5 = bf16[64,4,1024]{2,1,0:T(4,128)(2,1)} all-reduce(f32[64,4,1024]{2,1,0:T(4,128)S(1)} %copy.161), channel_id=2, replica_groups=mesh['streams'=16,'tp'=32] {'tp'}, use_global_device_ids=true, to_apply=%region_11.12.clone | all-reduce | flops 262144 | bytes 1572864
  529.9 0.7 dynamic-slice_convert_fusion
  530.6 49.6 %all_gather.15 = bf16[32,4,1024]{2,1,0:T(4,128)(2,1)S(1)} all-gather(bf16[2,4,1024]{2,1,0:T(4,128)(2,1)S(1)} %dynamic-slice_convert_fusion), channel_id=1, replica_groups=mesh['streams'=16,'tp'=32] {'streams'}, dimensions={0}, use_global_device_ids=true | all-gather | bytes 278528 | tf_op jit(solution)/shard_map/all_gather | solution.py:175
  (67 shorter events, 5.7 us)
Async XLA Ops:
  6.5 242.1 %copy-start = (bf16[8192,128]{1,0:T(8,128)(2,1)S(1)}, bf16[8192,128]{1,0:T(8,128)(2,1)}, u32[]{:S(2)}) copy-start(bf16[8192,128]{1,0:T(8,128)(2,1)} %param.23) | copy-start | bytes 6291460
  6.5 140.4 %copy-start.4 = (s32[1,4]{1,0:T(1,128)S(1)}, s32[1,4]{1,0:T(1,128)}, u32[]{:S(2)}) copy-start(s32[1,4]{1,0:T(1,128)} %param.18) | copy-start | bytes 52
  6.5 131.5 %all-gather.4.cloned.1.call-start = ((), (), s32[]{:S(2)}) async-start(), calls=%async_computation | async-start | bytes 4202496 | tf_op jit(solution)/shard_map/all_gather | solution.py:84
  6.5 234.3 %copy-start.7 = (f32[8192]{0:T(1024)S(1)}, f32[8192]{0:T(1024)}, u32[]{:S(2)}) copy-start(f32[8192]{0:T(1024)} %param.22) | copy-start | bytes 98308
  6.6 236.4 %copy-start.6 = (s32[1,64]{1,0:T(1,128)S(1)}, s32[1,64]{1,0:T(1,128)}, u32[]{:S(2)}) copy-start(s32[1,64]{1,0:T(1,128)} %param.27) | copy-start | bytes 772
  6.6 236.5 %copy-start.2 = (bf16[256,1024]{1,0:T(8,128)(2,1)S(1)}, bf16[256,1024]{1,0:T(8,128)(2,1)}, u32[]{:S(2)}) copy-start(bf16[256,1024]{1,0:T(8,128)(2,1)} %param.24) | copy-start | bytes 1572868
  13.3 232.0 %all-gather.6.cloned.1.call-start = ((), (), s32[]{:S(2)}) async-start(), calls=%async_computation.1 | async-start | bytes 4325376 | tf_op jit(solution)/shard_map/all_gather | solution.py:109
  143.7 254.7 %all-reduce.4.cloned.1.call-start = ((), (), s32[]{:S(2)}) async-start(), calls=%async_computation.2 | async-start | bytes 2097152 | tf_op jit(solution)/shard_map/psum | solution.py:127
  245.4 3.5 copy-start.1
  250.1 153.9 %copy-start.3 = (bf16[128,1024]{1,0:T(8,128)(2,1)S(1)}, bf16[128,1024]{1,0:T(8,128)(2,1)}, u32[]{:S(2)}) copy-start(bf16[128,1024]{1,0:T(8,128)(2,1)} %param.25) | copy-start | bytes 786436
  401.5 178.7 %copy-start.5 = (bf16[1,1024]{1,0:T(2,128)(2,1)S(1)}, bf16[1,1024]{1,0:T(2,128)(2,1)}, u32[]{:S(2)}) copy-start(bf16[1,1024]{1,0:T(2,128)(2,1)} %param.19) | copy-start | bytes 6148
Sparse Core Ops, SparseCore 0:
  13.5 124.5 all-gather.3
  143.8 85.0 all-gather.5
  245.4 152.8 all-reduce.3
where the time goes:
time: 588 us; the launch traced here: 587 us
  waiting for transfers between devices  271 us (46%)
  blocking collectives  265 us (45%)
  between operations  18.6 us (3%)
  matrix products  15 us (3%)
  other arithmetic  9.66 us (2%)
  local copies, waits for them, and re-layouts  7.67 us (1%)
    psum x1, waiting for transfers between devices, coarse_project(): keyvals = lax.psum(keyval_part, 'tp')  148 us
    unnamed x1, blocking collectives  125 us
    all_gather x1, waiting for transfers between devices, dispatch(): lax.all_gather(block_rows, ('streams', 'tp'), axis=0, tiled=True)  123 us
    all_gather x1, blocking collectives, dispatch(): lax.all_gather(block_marks, ('streams', 'tp'), axis=0, tiled=True)  90.5 us
    all_gather x1, blocking collectives, give_back(): every_back = lax.all_gather(summed, 'streams', axis=0, tiled=True)  49.6 us
  transfers between devices with their start and end apart: 3, of which 2 were waited for; matrix products, arithmetic and copies ran while one was open for 2% of the time, Pallas kernels for 0%

commit v1 on v0

--- a/solution.py
+++ b/solution.py
@@ -124,7 +124,7 @@
     keyval_part = jnp.einsum(
         "rbf,fc->rbc", own_scaled, keyval_weight, preferred_element_type=jnp.float32
     )
-    keyvals = lax.psum(keyval_part, "tp")
+    keyvals = jnp.sum(lax.all_gather(keyval_part, "tp"), axis=0)
     new_keys = (lax.dynamic_slice_in_dim(keyvals, head_group * HD, HD, 2) * inverse).astype(
         jnp.bfloat16
     )

time: 588 us -> 668 us (1.14)
  waiting for transfers between devices: 271 us -> 343 us
  other arithmetic: 9.66 us -> 21.5 us
    all_gather x0 -> x1, waiting for transfers between devices: none -> 220 us  [coarse_project(): keyvals = jnp.sum(lax.all_gather(keyval_part, 'tp'), axis=0)]
    psum x1 -> x0, waiting for transfers between devices: 148 us -> none  [coarse_project(): keyvals = lax.psum(keyval_part, 'tp')]
    reduce_sum x0 -> x1, other arithmetic: none -> 11.9 us  [coarse_project(): keyvals = jnp.sum(lax.all_gather(keyval_part, 'tp'), axis=0)]
where the time goes in v1:
time: 668 us
  waiting for transfers between devices  343 us (51%)
  blocking collectives  261 us (39%)
  other arithmetic  21.5 us (3%)
  between operations  18.6 us (3%)
  matrix products  15.4 us (2%)
  local copies, waits for them, and re-layouts  8.17 us (1%)
    all_gather x1, waiting for transfers between devices, coarse_project(): keyvals = jnp.sum(lax.all_gather(keyval_part, 'tp'), axis=0)  220 us
    unnamed x1, blocking collectives  123 us
    all_gather x1, waiting for transfers between devices, dispatch(): lax.all_gather(block_rows, ('streams', 'tp'), axis=0, tiled=True)  123 us
    all_gather x1, blocking collectives, dispatch(): lax.all_gather(block_marks, ('streams', 'tp'), axis=0, tiled=True)  91.3 us
    all_gather x1, blocking collectives, give_back(): every_back = lax.all_gather(summed, 'streams', axis=0, tiled=True)  45.8 us
  transfers between devices with their start and end apart: 3, of which 2 were waited for; matrix products, arithmetic and copies ran while one was open for 2% of the time, Pallas kernels for 0%

profile of v1, /device:TPU:1, one launch (start us, length us, event | category | flops | bytes accessed | tf_op | source)
XLA Modules:
  0.0 667.7 jit_solution(615386057321906401)
XLA Ops:
  6.6 0.9 slice.62
  7.4 0.9 convolution_multiply_fusion.2
  8.3 1.0 fusion.96
  11.1 0.9 fusion.32
  12.0 0.7 fusion.61
  13.4 0.9 convert_reduce_fusion
  14.3 0.7 select_bitcast_fusion
  15.1 122.9 %all-gather.6.cloned.1.call-done = bf16[512,4,1024]{2,1,0:T(4,128)(2,1)} async-done(((bf16[1,4,1024]{2,1,0:T(4,128)(2,1)}), bf16[512,4,1024]{2,1,0:T(4,128)(2,1)}) %all-gather.6.cloned.1.call-update) | async-done | bytes 4194320 | tf_op jit(solution)/shard_map/all_gather | solution.py:84
  138.0 5.7 fusion.14
  143.8 2.2 fusion.35
  146.7 1.2 fusion.100
  149.3 91.3 %all-gather.1 = bf16[512,1,4]{2,1,0:T(2,128)(2,1)S(1)} all-gather(bf16[1,1,4]{2,1,0:T(2,128)(2,1)S(1)} %convert_bitcast_fusion), channel_id=1, replica_groups=mesh['streams'=16,'tp'=32] {'streams','tp'}, dimensions={0}, use_global_device_ids=true | all-gather | bytes 4104 | tf_op jit(solution)/shard_map/all_gather | solution.py:85
  244.0 1.3 dynamic-slice.4
  246.2 3.3 fusion.1
  250.1 1.2 fusion.23
  251.4 1.0 fusion.99
  252.4 220.4 %all-gather.10.cloned.1.call-done = f32[2048,4,1024]{2,0,1:T(8,128)} async-done(((f32[64,4,1024]{2,0,1:T(8,128)}), f32[2048,4,1024]{2,0,1:T(8,128)}) %all-gather.10.cloned.1.call-update) | async-done | bytes 33554448 | tf_op jit(solution)/shard_map/all_gather | solution.py:127
  472.9 11.9 %reduce_sum.67 = f32[64,4,1024]{2,0,1:T(8,128)S(1)} reduce(f32[32,64,4,1024]{3,1,0,2:T(8,128)} %bitcast.185, f32[]{:T(128)} %constant.89.clone.1), dimensions={0}, to_apply=%region_7.8 | reduce | flops 8126464 | bytes 34603012 | tf_op jit(solution)/shard_map/reduce_sum | solution.py:127
  484.8 1.0 fusion.48
  486.5 1.1 fusion.44
  488.2 1.5 fusion.28
  490.6 123.4 %all-reduce.2 = bf16[64,4,1024]{2,1,0:T(4,128)(2,1)} all-reduce(f32[64,4,1024]{2,1,0:T(4,128)S(1)} %copy.161), channel_id=3, replica_groups=mesh['streams'=16,'tp'=32] {'tp'}, use_global_device_ids=true, to_apply=%region_11.12.clone | all-reduce | flops 262144 | bytes 1572864
  614.0 0.7 dynamic-slice_convert_fusion
  614.7 45.8 %all_gather.23 = bf16[32,4,1024]{2,1,0:T(4,128)(2,1)S(1)} all-gather(bf16[2,4,1024]{2,1,0:T(4,128)(2,1)S(1)} %dynamic-slice_convert_fusion), channel_id=1, replica_groups=mesh['streams'=16,'tp'=32] {'streams'}, dimensions={0}, use_global_device_ids=true | all-gather | bytes 278528 | tf_op jit(solution)/shard_map/all_gather | solution.py:175
  (72 shorter events, 7.2 us)
Async XLA Ops:
  6.5 243.0 %copy-start = (bf16[8192,128]{1,0:T(8,128)(2,1)S(1)}, bf16[8192,128]{1,0:T(8,128)(2,1)}, u32[]{:S(2)}) copy-start(bf16[8192,128]{1,0:T(8,128)(2,1)} %param.23) | copy-start | bytes 6291460
  6.5 137.2 %copy-start.7 = (f32[8192]{0:T(1024)S(1)}, f32[8192]{0:T(1024)}, u32[]{:S(2)}) copy-start(f32[8192]{0:T(1024)} %param.22) | copy-start | bytes 98308
  6.5 137.3 %copy-start.2 = (bf16[256,1024]{1,0:T(8,128)(2,1)S(1)}, bf16[256,1024]{1,0:T(8,128)(2,1)}, u32[]{:S(2)}) copy-start(bf16[256,1024]{1,0:T(8,128)(2,1)} %param.24) | copy-start | bytes 1572868
  6.5 131.5 %all-gather.6.cloned.1.call-start = ((), (), s32[]{:S(2)}) async-start(), calls=%async_computation | async-start | bytes 4202496 | tf_op jit(solution)/shard_map/all_gather | solution.py:84
  13.3 232.8 %all-gather.8.cloned.1.call-start = ((), (), s32[]{:S(2)}) async-start(), calls=%async_computation.1 | async-start | bytes 4325376 | tf_op jit(solution)/shard_map/all_gather | solution.py:109
  15.1 134.2 %copy-start.4 = (s32[1,4]{1,0:T(1,128)S(1)}, s32[1,4]{1,0:T(1,128)}, u32[]{:S(2)}) copy-start(s32[1,4]{1,0:T(1,128)} %param.18) | copy-start | bytes 52
  15.1 231.0 %copy-start.6 = (s32[1,64]{1,0:T(1,128)S(1)}, s32[1,64]{1,0:T(1,128)}, u32[]{:S(2)}) copy-start(s32[1,64]{1,0:T(1,128)} %param.27) | copy-start | bytes 772
  143.7 329.2 %all-gather.10.cloned.1.call-start = ((), (), s32[]{:S(2)}) async-start(), calls=%async_computation.2 | async-start | bytes 34603008 | tf_op jit(solution)/shard_map/all_gather | solution.py:127
  246.1 3.9 copy-start.1
  249.5 1.9 copy-start.8
  251.3 221.5 %copy-start.9 = (bf16[64,4,128]{2,0,1:T(8,128)(2,1)}, bf16[64,4,128]{2,0,1:T(8,128)(2,1)S(1)}, u32[]{:S(2)}) copy-start(bf16[64,4,128]{2,0,1:T(8,128)(2,1)S(1)} %fusion.23) | copy-start | bytes 196612
  472.9 16.8 %copy-start.3 = (bf16[128,1024]{1,0:T(8,128)(2,1)S(1)}, bf16[128,1024]{1,0:T(8,128)(2,1)}, u32[]{:S(2)}) copy-start(bf16[128,1024]{1,0:T(8,128)(2,1)} %param.25) | copy-start | bytes 786436
  485.9 174.6 %copy-start.5 = (bf16[1,1024]{1,0:T(2,128)(2,1)S(1)}, bf16[1,1024]{1,0:T(2,128)(2,1)}, u32[]{:S(2)}) copy-start(bf16[1,1024]{1,0:T(2,128)(2,1)} %param.19) | copy-start | bytes 6148
Sparse Core Ops, SparseCore 0:
  13.4 124.5 all-gather.5
  143.8 83.1 all-gather.7
  230.2 242.6 all-gather.9
